TPU v7x, 32 devices: a whole 2x2x4 slice. The times are simulated.
32 devices in a mesh: section: 4 (over z), dp: 8 (over y, x, core).
Axes of the slice: x: 2, y: 2, z: 4, core: 2. Of those that a mesh axis runs over, the one named last changes fastest.
Arguments:
- tokens: bfloat16 [2048, 4096], P('dp'), may hold values from -48 to 48
- orig_weight: bfloat16 [1024, 4096], P(('section', 'dp')), may hold values from -6 to 6
- keep_flags: int32 [64], replicated, may hold values from 0 to 1, as said below
Outputs:
- corrected: bfloat16 [1024, 4096], P(('section', 'dp'))
Inputs may be any that keep to these rules, and one draw needn't show every extreme that they name: `keep_flags`: exactly 12 of the 64 flags are 1.
All inputs are finite; a program needn't handle non-finite values.
Results may differ from a plain program's by a relative error of at most 0.003.
Values may be sent and summed in bfloat16 or wider, within the bound.
No kernel may reach another device: no remote copies, remote signals or barrier semaphores. Data moves between devices by JAX's collectives and lax.ppermute only.
A program may use at most 64 MiB of HBM per device.

v0:
```python
import functools

import jax
import jax.numpy as jnp
from jax import lax
from jax.experimental import pallas as pl
from jax.experimental.pallas import tpu as pltpu
from jax.sharding import PartitionSpec as P

KEEP_BLK = 12
PANEL = 128
SUB = 8
EXTRA = 16
VMEM_LIMIT = 32 * 1024 * 1024
NT = (((1,), (1,)), ((), ()))
NN = (((1,), (0,)), ((), ()))


def split3(x):
    hi = x.astype(jnp.bfloat16)
    rest = x - hi.astype(jnp.float32)
    mid = rest.astype(jnp.bfloat16)
    low = (rest - mid.astype(jnp.float32)).astype(jnp.bfloat16)
    return hi, mid, low


def dot32(a, b, dims):
    return lax.dot_general(a, b, dims, preferred_element_type=jnp.float32)


def kept_blocks(flags_ref, index_ref):
    count = jnp.int32(0)
    for b in range(flags_ref.shape[0]):
        index_ref[count] = b
        count = count + flags_ref[b]


def select_kernel(flags_ref, tokens_ref, out_ref, index_ref, held_ref, sem):
    rows, features = tokens_ref.shape
    blocks = flags_ref.shape[0]
    width = features // blocks
    per_tile = 128 // width
    chunks = sem.shape[0]
    step = rows // chunks
    reads = []
    for c in range(chunks):
        part = pl.ds(c * step, step)
        reads.append(pltpu.make_async_copy(tokens_ref.at[part, :], held_ref.at[part, :], sem.at[c]))
        reads[-1].start()
    kept_blocks(flags_ref, index_ref)
    row = lax.broadcasted_iota(jnp.int32, (width, 128), 0)
    lane = lax.broadcasted_iota(jnp.int32, (width, 128), 1)
    for copy in reads:
        copy.wait()
    for i in range(KEEP_BLK):
        b = index_ref[i]
        start = pl.multiple_of((b // per_tile) * 128, 128)
        pick = jnp.where(lane == row + (b % per_tile) * width, 1.0, 0.0).astype(jnp.bfloat16)
        picked = dot32(pick, held_ref[:, pl.ds(start, 128)], NT)
        out_ref[i * width:(i + 1) * width, :] = picked.astype(jnp.bfloat16)
    total = jnp.zeros((step, 128), jnp.float32)
    for c in range(chunks):
        for f in range(features // 128):
            piece = held_ref[c * step:(c + 1) * step, f * 128:(f + 1) * 128].astype(jnp.float32)
            total += piece * piece
    squares = jnp.sum(total)
    hi, mid, low = split3(jnp.full((EXTRA, rows), squares, jnp.float32))
    row = lax.broadcasted_iota(jnp.int32, (EXTRA, rows), 0)
    carried = jnp.where(
        row == 0,
        hi.astype(jnp.float32),
        jnp.where(row == 1, mid.astype(jnp.float32), jnp.where(row == 2, low.astype(jnp.float32), 0.0)),
    )
    out_ref[KEEP_BLK * width:, :] = carried.astype(jnp.bfloat16)


def select_kept(tokens, keep_flags):
    rows, features = tokens.shape
    blocks = keep_flags.shape[0]
    kept = KEEP_BLK * (features // blocks)
    chunks = 4
    return pl.pallas_call(
        select_kernel,
        out_shape=jax.ShapeDtypeStruct((kept + EXTRA, rows), jnp.bfloat16),
        in_specs=[
            pl.BlockSpec(memory_space=pltpu.SMEM),
            pl.BlockSpec(memory_space=pl.ANY),
        ],
        out_specs=pl.BlockSpec(memory_space=pltpu.VMEM),
        scratch_shapes=[
            pltpu.SMEM((blocks + 1,), jnp.int32),
            pltpu.VMEM((rows, features), jnp.bfloat16),
            pltpu.SemaphoreType.DMA((chunks,)),
        ],
        compiler_params=pltpu.CompilerParams(vmem_limit_bytes=VMEM_LIMIT),
        name="select_kept",
    )(keep_flags, tokens)


def lane_column(x, c):
    return jnp.broadcast_to(x[:, c:c + 1], (SUB, 128))


def sublane_row(x, t):
    return jnp.broadcast_to(x[t:t + 1, :], (SUB, 128))


def tree_sum(terms):
    while len(terms) > 1:
        pairs = [terms[i] + terms[i + 1] for i in range(0, len(terms) - 1, 2)]
        terms = pairs + terms[len(terms) - len(terms) % 2:]
    return terms[0]


def block_entries(block, base):
    entry = {}
    for j in range(SUB):
        column = lane_column(block, base + j)
        for i in range(j + 1):
            entry[i, j] = sublane_row(column, i)
    return entry


def solve_small(entry, rows, cross, ahead):
    entry, rows, cross, ahead = dict(entry), list(rows), list(cross), list(ahead)
    inverse = {}
    following = {}
    for t in range(0, SUB, 2):
        u = t + 1
        a, b, c = entry[t, t], entry[t, u], entry[u, u]
        first = pl.reciprocal(a, approx=True)
        second = a * pl.reciprocal(a * c - b * b, approx=True)
        step = b * first
        later = range(u + 1, SUB)
        one = {j: entry[t, j] * first for j in later}
        rest = {j: entry[u, j] - b * one[j] for j in later}
        for j in later:
            for i in range(u + 1, j + 1):
                partial = entry[i, j] - entry[t, i] * one[j]
                entry[i, j] = partial - (rest[i] * rest[j]) * second
        two = {j: rest[j] * second for j in later}
        if cross:
            cross[u] = cross[u] - step * cross[t]
            for j in later:
                cross[j] = (cross[j] - one[j] * cross[t]) - two[j] * cross[u]
            if u + 1 < SUB:
                left, right = cross[t] * first, cross[u] * second
                for j in range(SUB):
                    ahead[j] = (ahead[j] - left * sublane_row(cross[t], j)) - right * sublane_row(cross[u], j)
            else:
                left = [sublane_row(cross[t], j) for j in range(SUB)]
                right = [sublane_row(cross[u], j) for j in range(SUB)]
                for j in range(SUB):
                    for i in range(j + 1):
                        value = sublane_row(ahead[j], i) - (left[i] * left[j]) * first
                        following[i, j] = value - (right[i] * right[j]) * second
        rows[u] = rows[u] - step * rows[t]
        inverse[u, t] = -step
        for k in range(t):
            inverse[u, k] = inverse[u, k] - step * inverse[t, k]
        for j in later:
            rows[j] = (rows[j] - one[j] * rows[t]) - two[j] * rows[u]
            for k in range(t):
                inverse[j, k] = (inverse[j, k] - one[j] * inverse[t, k]) - two[j] * inverse[u, k]
            inverse[j, t] = -one[j] - two[j] * inverse[u, t]
            inverse[j, u] = -two[j]
        rows[t] = rows[t] * first
        rows[u] = rows[u] * second
    rows = [
        tree_sum([rows[i]] + [inverse[j, i] * rows[j] for j in range(i + 1, SUB)]) for i in range(SUB)
    ]
    return rows, following


def invert_panel(block, beside=()):
    size = block.shape[0]
    count = size // SUB
    sub = lax.broadcasted_iota(jnp.int32, (SUB, 128), 0)
    lane = lax.broadcasted_iota(jnp.int32, (SUB, 128), 1)
    rows = [block[i * SUB:(i + 1) * SUB, :] for i in range(count)]
    entry = block_entries(rows[0], 0)
    done = 0
    for s in range(count):
        base = s * SUB
        inside = (lane >= base) & (lane < base + SUB)
        cross, ahead = [], []
        if s + 1 < count:
            cross = [lane_column(rows[s + 1], base + j) for j in range(SUB)]
            ahead = [lane_column(rows[s + 1], base + SUB + j) for j in range(SUB)]
        pivot_rows = jnp.where(inside, jnp.where(lane == sub + base, 1.0, 0.0), rows[s])
        spread, entry = solve_small(entry, [sublane_row(pivot_rows, j) for j in range(SUB)], cross, ahead)
        for i in [(s + d) % count for d in range(1, count)]:
            columns = cross if i == s + 1 else [lane_column(rows[i], base + j) for j in range(SUB)]
            change = tree_sum([columns[j] * spread[j] for j in range(SUB)])
            rows[i] = jnp.where(inside, 0.0, rows[i]) - change
        new = spread[SUB - 1]
        for j in range(SUB - 1):
            new = jnp.where(sub == j, spread[j], new)
        rows[s] = new
        until = len(beside) * (s + 1) // count
        for task in beside[done:until]:
            task()
        done = until
    return jnp.concatenate(rows, axis=0)


def wide_left(x):
    hi, mid, low = split3(x)
    return jnp.concatenate([hi, hi, mid, hi, mid, low], axis=1)


def wide_right(x):
    hi, mid, low = split3(x)
    return jnp.concatenate([hi, mid, hi, low, mid, hi], axis=0)


def spans(low, high):
    first = low + (high - low) % 256
    starts = ([low] if first > low else []) + list(range(first, high, 256))
    return list(zip(starts, starts[1:] + [high]))


def settle_tasks(p, state):
    a_ref, wide_ref, _, w_ref, left_ref, right_ref = state
    kept = a_ref.shape[0]
    at = p * PANEL
    low = at + PANEL
    here = slice(at, low)

    def make_w(c, d):
        value = dot32(wide_ref[...], wide_right(a_ref[here, c:d]), NN)
        w_ref[:, c:d] = value
        right_ref[:, c:d] = wide_right(value)

    def make_left():
        left_ref[low:, :] = wide_left(a_ref[low:, here])

    def update(c, d):
        a_ref[low:, c:d] -= dot32(left_ref[low:, :], right_ref[:, c:d], NN)

    def place():
        a_ref[here, low:] = w_ref[:, low:]

    tasks = [functools.partial(make_w, c, d) for c, d in spans(low, kept)] + [make_left]
    return tasks + [functools.partial(update, c, d) for c, d in spans(low, kept)] + [place]


def panel(p, state, pivot_ref, beside):
    a_ref, wide_ref, next_ref = state[:3]
    here, after = slice(p * PANEL, (p + 1) * PANEL), slice((p + 1) * PANEL, (p + 2) * PANEL)
    inverse = invert_panel(next_ref[...], beside)
    wide = wide_left(inverse)
    crossing = dot32(wide, wide_right(a_ref[here, after]), NN)
    next_ref[...] = a_ref[after, after] - dot32(wide_left(a_ref[after, here]), wide_right(crossing), NN)
    pivot_ref[...] = inverse
    wide_ref[...] = wide


def place_pieces(pieces, all_ref, sem):
    copies = []
    at = 0
    for k, piece in enumerate(pieces):
        width = piece.shape[1]
        copies.append(pltpu.make_async_copy(piece, all_ref.at[:, at:at + width], sem.at[k]))
        copies[-1].start()
        at += width
    return copies


def first_kernel(features, rows, last, *refs):
    pieces, refs = refs[:-9], refs[-9:]
    a_ref, scale_ref, pivot_ref, wide_ref, next_ref, all_ref, w_ref, left_ref, right_ref = refs
    kept = a_ref.shape[0]
    tokens = all_ref.shape[1]
    total = jnp.float32(0.0)
    for k in range(0, tokens, rows):
        total = total + jnp.sum(all_ref[kept:, k:k + 1].astype(jnp.float32))
    scale_ref[...] = 1.0 / jnp.full(scale_ref.shape, 0.01 * total / features, jnp.float32)
    scale = scale_ref[0:1, 0:1]
    chunk = 2048 if tokens % 2048 == 0 else rows

    def gram(at, tile):
        row = lax.broadcasted_iota(jnp.int32, (kept, tile), 0)
        lane = lax.broadcasted_iota(jnp.int32, (kept, tile), 1)
        acc = jnp.where(row == lane + at, 1.0, 0.0)
        for c in range(0, tokens, chunk):
            part = dot32(all_ref[:kept, c:c + chunk], all_ref[at:at + tile, c:c + chunk], NT)
            acc = acc + part * scale
        a_ref[:, at:at + tile] = acc

    gram(0, 256)
    next_ref[...] = a_ref[:PANEL, :PANEL]
    state = (a_ref, wide_ref, next_ref, w_ref, left_ref, right_ref)
    for p in range(last):
        if p:
            tasks = settle_tasks(p - 1, state)
        else:
            tasks = [functools.partial(gram, at, 256) for at in range(256, kept, 256)]
        panel(p, state, pivot_ref.at[p], tasks)


def first_half(pieces, features, last):
    kept_extra, rows = pieces[0].shape
    kept = kept_extra - EXTRA
    count = len(pieces)
    tokens = sum(piece.shape[1] for piece in pieces)

    def body(*refs):
        refs, sem = refs[:-1], refs[-1]
        for copy in place_pieces(refs[:count], refs[count + 5], sem):
            copy.wait()
        first_kernel(float(features), rows, last, *refs)

    return pl.pallas_call(
        body,
        out_shape=[
            jax.ShapeDtypeStruct((kept, kept), jnp.float32),
            jax.ShapeDtypeStruct((8, 128), jnp.float32),
            jax.ShapeDtypeStruct((last, PANEL, PANEL), jnp.float32),
            jax.ShapeDtypeStruct((PANEL, 6 * PANEL), jnp.bfloat16),
            jax.ShapeDtypeStruct((PANEL, PANEL), jnp.float32),
        ],
        in_specs=[pl.BlockSpec(memory_space=pl.ANY)] * count,
        out_specs=[pl.BlockSpec(memory_space=pltpu.VMEM)] * 5,
        scratch_shapes=[
            pltpu.VMEM((kept_extra, tokens), jnp.bfloat16),
            pltpu.VMEM((PANEL, kept), jnp.float32),
            pltpu.VMEM((kept, 6 * PANEL), jnp.bfloat16),
            pltpu.VMEM((6 * PANEL, kept), jnp.bfloat16),
            pltpu.SemaphoreType.DMA((count,)),
        ],
        compiler_params=pltpu.CompilerParams(vmem_limit_bytes=VMEM_LIMIT),
        name="gram_and_first_panels",
    )(*pieces)


def dot_small(x, y, dims=NN):
    rows = x.shape[0]
    hi, mid, low = split3(x)
    yhi, ymid, ylow = split3(y)
    first = dot32(jnp.concatenate([hi, mid, low], axis=0), yhi, dims)
    second = dot32(jnp.concatenate([hi, mid], axis=0), ymid, dims)
    third = dot32(hi, ylow, dims)
    small = first[2 * rows:] + second[rows:] + third
    return small + (first[rows:2 * rows] + second[:rows]) + first[:rows]


def second_kernel(chips, first, copies, flags_ref, *refs):
    projected, refs = refs[:chips], refs[chips:]
    start_ref, early_ref, start_wide_ref, start_next_ref, scale_ref = refs[:5]
    out_ref, index_ref, wide_out_ref, all_ref, late_ref = refs[-11:-6]
    state = refs[-6:]
    a_ref, wide_ref, next_ref = state[:3]
    own, features = out_ref.shape
    blocks = flags_ref.shape[0]
    width = features // blocks
    per_tile = 128 // width
    kept = a_ref.shape[0]
    last = kept // PANEL - 1
    at = last * PANEL
    kept_blocks(flags_ref, index_ref)
    wide_out_ref[...] = jnp.zeros((own, features), jnp.float32)
    live = (first - 1) * PANEL
    a_ref[live:, live:] = start_ref[live:, live:]
    wide_ref[...] = start_wide_ref[...]
    next_ref[...] = start_next_ref[...]
    held = {}

    def block(p):
        return slice(p * PANEL, (p + 1) * PANEL)

    def factor(p):
        return (start_ref if p < first - 1 else a_ref)[block(p), (p + 1) * PANEL:]

    def pivot(p):
        return early_ref[p] if p < first else late_ref[p - first]

    def make_right():
        whole = jnp.concatenate([part[...] for part in projected], axis=1)
        right = dot32(jnp.concatenate(split3(whole), axis=0), all_ref[:kept, :], NT)
        held["right"] = right[:own] + right[own:2 * own] + right[2 * own:]

    def forward(p):
        right = held["right"]
        held["z", p] = right[:, :PANEL]
        held["right"] = right[:, PANEL:] - dot_small(right[:, :PANEL], factor(p))

    def scaled(p):
        held["zd", p] = dot_small(held["z", p], pivot(p))

    def backward(p):
        if p == last:
            row = lax.broadcasted_iota(jnp.int32, (own + PANEL, PANEL), 0)
            lane = lax.broadcasted_iota(jnp.int32, (own + PANEL, PANEL), 1)
            held["back"] = jnp.where(row == lane + own, 1.0, 0.0)
        else:
            base = jnp.concatenate([held["zd", p], jnp.zeros((PANEL, PANEL), jnp.float32)], axis=0)
            value = base - dot_small(held["back"], factor(p), NT)
            held["back"] = jnp.concatenate([value, held["back"]], axis=1)

    for p in range(first, last):
        tasks = settle_tasks(p - 1, state)
        if p == last - 1:
            for copy in copies:
                copy.wait()
            tasks = [make_right] + [functools.partial(forward, q) for q in range(p - 1)] + tasks
            tasks += [functools.partial(forward, p - 1)] + [functools.partial(scaled, q) for q in range(p)]
        panel(p, state, late_ref.at[p - first], tasks)
    tasks = settle_tasks(last - 1, state)
    tasks += [functools.partial(forward, last - 1), functools.partial(scaled, last - 1)]
    tasks += [functools.partial(backward, p) for p in reversed(range(last + 1))]
    inverse = invert_panel(next_ref[...], tasks)
    tail = dot_small(held["right"], inverse)
    scale = scale_ref[0:1, 0:1]
    front = held["back"][:own, :at] + dot_small(tail, held["back"][own:, :at])
    answer = [front[:, c:c + PANEL] * scale for c in range(0, at, PANEL)] + [tail * scale]
    place = lax.broadcasted_iota(jnp.int32, (own, 128), 1) // width
    for i in range(KEEP_BLK):
        b = index_ref[i]
        start = pl.multiple_of((b // per_tile) * 128, 128)
        inner = b % per_tile
        source = answer[i // per_tile]
        moved = pltpu.roll(source, width, 1)
        value = jnp.where(inner == i % per_tile, source, moved)
        old = wide_out_ref[:, pl.ds(start, 128)]
        wide_out_ref[:, pl.ds(start, 128)] = jnp.where(place == inner, value, old)
    out_ref[...] = wide_out_ref[...].astype(jnp.bfloat16)


def second_half(keep_flags, projected, begun, scale, pieces, features, first):
    own = projected[0].shape[0]
    blocks = keep_flags.shape[0]
    chips = len(projected)
    kept = begun[0].shape[0]
    count = len(pieces)
    tokens = sum(piece.shape[1] for piece in pieces)
    vmem = pl.BlockSpec(memory_space=pltpu.VMEM)
    anywhere = pl.BlockSpec(memory_space=pl.ANY)

    def body(*refs):
        refs, sem = refs[:-1], refs[-1]
        ins = 6 + chips
        copies = place_pieces(refs[ins:ins + count], refs[ins + count + 3], sem)
        second_kernel(chips, first, copies, *refs)

    return pl.pallas_call(
        body,
        out_shape=jax.ShapeDtypeStruct((own, features), jnp.bfloat16),
        in_specs=[pl.BlockSpec(memory_space=pltpu.SMEM)] + [vmem] * (chips + 5) + [anywhere] * count,
        out_specs=vmem,
        scratch_shapes=[
            pltpu.SMEM((blocks + 1,), jnp.int32),
            pltpu.VMEM((own, features), jnp.float32),
            pltpu.VMEM((kept + EXTRA, tokens), jnp.bfloat16),
            pltpu.VMEM((kept // PANEL - 1 - first, PANEL, PANEL), jnp.float32),
            pltpu.VMEM((kept, kept), jnp.float32),
            pltpu.VMEM((PANEL, 6 * PANEL), jnp.bfloat16),
            pltpu.VMEM((PANEL, PANEL), jnp.float32),
            pltpu.VMEM((PANEL, kept), jnp.float32),
            pltpu.VMEM((kept, 6 * PANEL), jnp.bfloat16),
            pltpu.VMEM((6 * PANEL, kept), jnp.bfloat16),
            pltpu.SemaphoreType.DMA((count,)),
        ],
        compiler_params=pltpu.CompilerParams(vmem_limit_bytes=VMEM_LIMIT),
        name="last_panels_and_solution",
    )(keep_flags, *projected, *begun, scale, *pieces)


def solution(mesh):
    n = mesh.shape["dp"]
    others = range(2, n, 2)

    def swap(x, k):
        return lax.ppermute(x, "dp", [(d, d ^ k) for d in range(n)])

    def gather_kept(kept):
        if n != 8:
            same = [kept] + [swap(kept, k) for k in others]
            return [part for piece in same for part in (piece, swap(piece, 1))], same[-1]
        near = [swap(kept, 2), swap(kept, 4)]
        sibling = swap(kept, 1)
        near, sibling = lax.optimization_barrier((near, sibling))
        middle = kept.shape[1] // 2
        far = [swap(near[0][:, :middle], 4), swap(near[1][:, middle:], 2)]
        near_sibling = [swap(piece, 1) for piece in near]
        far, near_sibling = lax.optimization_barrier((far, near_sibling))
        pieces = [kept, sibling, near[0], near_sibling[0], near[1], near_sibling[1]]
        return pieces + far + [swap(piece, 1) for piece in far], far

    def on_device(tokens, orig_weight, keep_flags):
        features = tokens.shape[1]
        own = orig_weight.shape[0]
        kept = select_kept(tokens, keep_flags)
        panels = (kept.shape[0] - EXTRA) // PANEL
        half = panels // 2
        pieces, arrived = gather_kept(kept)
        orig_weight, arrived = lax.optimization_barrier((orig_weight, arrived))
        sibling = swap(tokens, 1)
        weights = [orig_weight] + [swap(orig_weight, k) for k in others]
        a, scale, *state = first_half(pieces, features, half)
        a, weights, sibling = lax.optimization_barrier((a, weights, sibling))
        stacked = jnp.concatenate(weights, axis=0)
        projected = [
            lax.dot_general(stacked, part, NT, preferred_element_type=jnp.float32) for part in (tokens, sibling)
        ]
        projected = lax.optimization_barrier(jnp.concatenate(projected, axis=1))
        parts = [projected[i * own:(i + 1) * own] for i in range(n // 2)]
        parts = [parts[0]] + [swap(part, k) for part, k in zip(parts[1:], others)]
        return second_half(keep_flags, parts, (a, *state), scale, pieces, features, half)

    in_specs = (P("dp", None), P(("section", "dp"), None), P())
    out_specs = P(("section", "dp"), None)
    return jax.shard_map(on_device, mesh=mesh, in_specs=in_specs, out_specs=out_specs, check_vma=False)
```

profile of v0, /device:TPU:0, one launch (start us, length us, event | category | flops | bytes accessed | tf_op | source)
XLA Modules:
  0.0 74.6 jit_solution(6558559899106178149)
XLA Ops:
  0.0 0.5 collective-permute-start.12
  0.5 0.0 copy-start
  0.5 1.6 %copy-done = bf16[256,4096]{1,0:T(8,128)(2,1)S(1)} copy-done((bf16[256,4096]{1,0:T(8,128)(2,1)S(1)}, bf16[256,4096]{1,0:T(8,128)(2,1)}, u32[]{:S(2)}) %copy-start) | copy-done | bytes 2097176
  2.0 0.0 copy-start.2
  2.0 0.7 copy-done.2
  2.7 0.0 copy-start.3
  2.7 1.6 %select_kept.1.refs_0_.refs_10_ = bf16[784,256]{1,0:T(8,128)(2,1)S(1)} custom-call(s32[64]{0:T(128)S(1)} %copy-done.2, bf16[256,4096]{1,0:T(8,128)(2,1)S(1)} %copy-done), custom_call_target="tpu_custom_call" | custom-call | tf_op jit(solution)/shard_map/select_kept/pallas_call | solution.py:82
  4.3 0.1 collective-permute-start.2
  4.4 3.0 %collective-permute-start.1 = (bf16[784,256]{1,0:T(8,128)(2,1)S(1)}, bf16[784,256]{1,0:T(8,128)(2,1)S(1)}, u32[]{:S(2)}, u32[]{:S(2)}) collective-permute-start(bf16[784,256]{1,0:T(8,128)(2,1)S(1)} %select_kept.1.refs_0_.refs_10_), channel_id=1, source_target_pairs={{0,4},{1,5},{2,6},{3,7},{4,0},{5,1},{6,2},{7,3},{8,12},{9,13},{10,... | collective-permute-start | bytes 1204232 | tf_op jit(solution)/shard_map/ppermute | solution.py:474
  7.4 1.5 %collective-permute-start = (bf16[784,256]{1,0:T(8,128)(2,1)S(1)}, bf16[784,256]{1,0:T(8,128)(2,1)S(1)}, u32[]{:S(2)}, u32[]{:S(2)}) collective-permute-start(bf16[784,256]{1,0:T(8,128)(2,1)S(1)} %select_kept.1.refs_0_.refs_10_), channel_id=1, source_target_pairs={{0,2},{1,3},{2,0},{3,1},{4,6},{5,7},{6,4},{7,5},{8,10},{9,11},{10,... | collective-permute-start | bytes 1204232 | tf_op jit(solution)/shard_map/ppermute | solution.py:474
  8.9 0.0 collective-permute-done.2.refs_1_.refs_11_
  8.9 8.0 %collective-permute-done.1.refs_4_.refs_14_ = bf16[784,256]{1,0:T(8,128)(2,1)S(1)} collective-permute-done((bf16[784,256]{1,0:T(8,128)(2,1)S(1)}, bf16[784,256]{1,0:T(8,128)(2,1)S(1)}, u32[]{:S(2)}, u32[]{:S(2)}) %collective-permute-start.1) | collective-permute-done | bytes 401440 | tf_op jit(solution)/shard_map/ppermute | solution.py:474
  16.9 1.5 %collective-permute-done.refs_2_.refs_12_ = bf16[784,256]{1,0:T(8,128)(2,1)S(1)} collective-permute-done((bf16[784,256]{1,0:T(8,128)(2,1)S(1)}, bf16[784,256]{1,0:T(8,128)(2,1)S(1)}, u32[]{:S(2)}, u32[]{:S(2)}) %collective-permute-start) | collective-permute-done | bytes 401440 | tf_op jit(solution)/shard_map/ppermute | solution.py:474
  18.4 0.0 collective-permute-start.5
  18.4 0.5 collective-permute-start.6
  18.9 0.0 copy-start.1
  18.9 1.6 %collective-permute-start.4 = (bf16[784,128]{1,0:T(8,128)(2,1)S(1)}, bf16[784,128]{1,0:T(8,128)(2,1)S(1)}, u32[]{:S(2)}, u32[]{:S(2)}) collective-permute-start(bf16[784,128]{1,0:T(8,128)(2,1)S(1)} %slice.19), channel_id=1, source_target_pairs={{0,2},{1,3},{2,0},{3,1},{4,6},{5,7},{6,4},{7,5},{8,10},{9,11},{10,... | collective-permute-start | bytes 602120 | tf_op jit(solution)/shard_map/ppermute | solution.py:474
  20.5 0.5 collective-permute-start.3
  21.0 4.9 %collective-permute-done.4.refs_7_.refs_17_ = bf16[784,128]{1,0:T(8,128)(2,1)S(1)} collective-permute-done((bf16[784,128]{1,0:T(8,128)(2,1)S(1)}, bf16[784,128]{1,0:T(8,128)(2,1)S(1)}, u32[]{:S(2)}, u32[]{:S(2)}) %collective-permute-start.4) | collective-permute-done | bytes 200736 | tf_op jit(solution)/shard_map/ppermute | solution.py:474
  25.9 1.2 %collective-permute-done.3.refs_6_.refs_16_ = bf16[784,128]{1,0:T(8,128)(2,1)S(1)} collective-permute-done((bf16[784,128]{1,0:T(8,128)(2,1)S(1)}, bf16[784,128]{1,0:T(8,128)(2,1)S(1)}, u32[]{:S(2)}, u32[]{:S(2)}) %collective-permute-start.3) | collective-permute-done | bytes 200736 | tf_op jit(solution)/shard_map/ppermute | solution.py:474
  27.1 0.0 collective-permute-done.5.refs_3_.refs_13_
  27.1 0.0 collective-permute-done.6.refs_5_.refs_15_
  27.1 0.0 collective-permute-start.7
  27.1 0.0 copy-done.3
  27.1 0.4 collective-permute-start.11
  27.6 1.7 %collective-permute-start.10 = (bf16[32,4096]{1,0:T(8,128)(2,1)S(1)}, bf16[32,4096]{1,0:T(8,128)(2,1)S(1)}, u32[]{:S(2)}, u32[]{:S(2)}) collective-permute-start(bf16[32,4096]{1,0:T(8,128)(2,1)S(1)} %copy-done.3), channel_id=1, source_target_pairs={{0,4},{1,5},{2,6},{3,7},{4,0},{5,1},{6,2},{7,3},{8,12},{9,13},{10,... | collective-permute-start | bytes 786440 | tf_op jit(solution)/shard_map/ppermute | solution.py:474
  29.2 1.5 %collective-permute-start.9 = (bf16[32,4096]{1,0:T(8,128)(2,1)S(1)}, bf16[32,4096]{1,0:T(8,128)(2,1)S(1)}, u32[]{:S(2)}, u32[]{:S(2)}) collective-permute-start(bf16[32,4096]{1,0:T(8,128)(2,1)S(1)} %copy-done.3), channel_id=1, source_target_pairs={{0,2},{1,3},{2,0},{3,1},{4,6},{5,7},{6,4},{7,5},{8,10},{9,11},{10,... | collective-permute-start | bytes 786440 | tf_op jit(solution)/shard_map/ppermute | solution.py:474
  30.7 0.0 collective-permute-done.7.refs_8_.refs_18_
  30.7 0.0 collective-permute-start.8
  30.7 1.4 %collective-permute-done.8.refs_9_.refs_19_ = bf16[784,128]{1,0:T(8,128)(2,1)S(1)} collective-permute-done((bf16[784,128]{1,0:T(8,128)(2,1)S(1)}, bf16[784,128]{1,0:T(8,128)(2,1)S(1)}, u32[]{:S(2)}, u32[]{:S(2)}) %collective-permute-start.8) | collective-permute-done | bytes 200736 | tf_op jit(solution)/shard_map/ppermute | solution.py:474
  32.1 17.1 %gram_and_first_panels.1 = (f32[768,768]{1,0:T(8,128)S(1)}, f32[8,128]{1,0:T(8,128)S(1)}, f32[3,128,128]{2,1,0:T(8,128)S(1)}, bf16[128,768]{1,0:T(8,128)(2,1)S(1)}, f32[128,128]{1,0:T(8,128)S(1)}) custom-call(bf16[784,256]{1,0:T(8,128)(2,1)S(1)} %select_kept.1.refs_0_.refs_10_, bf16[784,256]{1,0:T(8,128)(2,1)S(1)} %collective-permute-done.2.refs_1_.refs_11_, ...), custom_call_target="tpu_custom_call" | custom-call | tf_op jit(solution)/shard_map/gram_and_first_panels/pallas_call | solution.py:314
  49.2 0.0 collective-permute-done.11
  49.2 0.0 collective-permute-done.10
  49.3 0.0 collective-permute-done.9
  49.3 0.0 collective-permute-done.12
  49.4 0.0 copy-done.1
  49.4 0.9 %fusion.1 = f32[128,256]{1,0:T(8,128)S(1)} fusion(bf16[128,4096]{1,0:T(8,128)(2,1)S(1)} %constant_dynamic-update-slice_fusion, bf16[256,4096]{1,0:T(8,128)(2,1)S(1)} %copy-done.1), kind=kOutput, calls=%fused_computation.6 | convolution fusion | flops 268435456 | bytes 3276800 | tf_op jit(solution)/shard_map/dot_general | solution.py:504
  50.3 0.8 %fusion.2 = f32[128,256]{1,0:T(8,128)S(1)} fusion(bf16[128,4096]{1,0:T(8,128)(2,1)S(1)} %constant_dynamic-update-slice_fusion, bf16[256,4096]{1,0:T(8,128)(2,1)S(1)} %collective-permute-done.12), kind=kOutput, calls=%fused_computation.7 | convolution fusion | flops 268435456 | bytes 3276800 | tf_op jit(solution)/shard_map/dot_general | solution.py:504
  51.2 0.4 collective-permute-start.15
  51.6 1.7 %collective-permute-start.14 = (f32[32,512]{1,0:T(8,128)S(1)}, f32[32,512]{1,0:T(8,128)S(1)}, u32[]{:S(2)}, u32[]{:S(2)}) collective-permute-start(f32[32,512]{1,0:T(8,128)S(1)} %get-tuple-element.44), channel_id=1, source_target_pairs={{0,4},{1,5},{2,6},{3,7},{4,0},{5,1},{6,2},{7,3},{8,12},{9,13},{10,... | collective-permute-start | bytes 196616 | tf_op jit(solution)/shard_map/ppermute | solution.py:474
  53.2 1.5 %collective-permute-start.13 = (f32[32,512]{1,0:T(8,128)S(1)}, f32[32,512]{1,0:T(8,128)S(1)}, u32[]{:S(2)}, u32[]{:S(2)}) collective-permute-start(f32[32,512]{1,0:T(8,128)S(1)} %get-tuple-element.45), channel_id=1, source_target_pairs={{0,2},{1,3},{2,0},{3,1},{4,6},{5,7},{6,4},{7,5},{8,10},{9,11},{10,... | collective-permute-start | bytes 196616 | tf_op jit(solution)/shard_map/ppermute | solution.py:474
  54.7 2.2 %collective-permute-done.15.refs_4_ = f32[32,512]{1,0:T(8,128)S(1)} collective-permute-done((f32[32,512]{1,0:T(8,128)S(1)}, f32[32,512]{1,0:T(8,128)S(1)}, u32[]{:S(2)}, u32[]{:S(2)}) %collective-permute-start.15) | collective-permute-done | bytes 65568 | tf_op jit(solution)/shard_map/ppermute | solution.py:474
  57.0 0.0 collective-permute-done.14.refs_3_
  57.0 0.5 collective-permute-done.13.refs_2_
  57.5 16.9 %last_panels_and_solution.1 = bf16[32,4096]{1,0:T(8,128)(2,1)} custom-call(s32[64]{0:T(128)S(1)} %copy-done.2, f32[32,512]{1,0:T(8,128)S(1)} %get-tuple-element.46.refs_1_, f32[32,512]{1,0:T(8,128)S(1)} %collective-permute-done.13.refs_2_, f32[32,512]{1,0:T(8,128)S(1)} %collective-permute-done.14.refs_3_, f32[32,512]{1,0:T(8,128)S(1)} %collective-permute-done.15.refs_4_, ...), custom_call_target="tpu_custom_call" | custom-call | tf_op jit(solution)/shard_map/last_panels_and_solution/pallas_call | solution.py:446
  (8 shorter events, 0.1 us)
Async XLA Ops:
  0.0 49.3 %collective-permute-start.12 = (bf16[256,4096]{1,0:T(8,128)(2,1)}, bf16[256,4096]{1,0:T(8,128)(2,1)S(1)}, u32[]{:S(2)}, u32[]{:S(2)}) collective-permute-start(bf16[256,4096]{1,0:T(8,128)(2,1)} %tokens_ref.1), channel_id=1, source_target_pairs={{0,1},{1,0},{2,3},{3,2},{4,5},{5,4},{6,7},{7,6},{8,9},{9,8},{10,11... | collective-permute-start | bytes 6291464 | tf_op jit(solution)/shard_map/ppermute | solution.py:474
  0.5 1.6 %copy-start = (bf16[256,4096]{1,0:T(8,128)(2,1)S(1)}, bf16[256,4096]{1,0:T(8,128)(2,1)}, u32[]{:S(2)}) copy-start(bf16[256,4096]{1,0:T(8,128)(2,1)} %tokens_ref.1) | copy-start | bytes 6291460
  2.0 0.7 copy-start.2
  2.7 24.4 %copy-start.3 = (bf16[32,4096]{1,0:T(8,128)(2,1)S(1)}, bf16[32,4096]{1,0:T(8,128)(2,1)}, u32[]{:S(2)}) copy-start(bf16[32,4096]{1,0:T(8,128)(2,1)} %param.4) | copy-start | bytes 786436
  4.3 4.6 %collective-permute-start.2 = (bf16[784,256]{1,0:T(8,128)(2,1)S(1)}, bf16[784,256]{1,0:T(8,128)(2,1)S(1)}, u32[]{:S(2)}, u32[]{:S(2)}) collective-permute-start(bf16[784,256]{1,0:T(8,128)(2,1)S(1)} %select_kept.1.refs_0_.refs_10_), channel_id=1, source_target_pairs={{0,1},{1,0},{2,3},{3,2},{4,5},{5,4},{6,7},{7,6},{8,9},{9,8},{10,11... | collective-permute-start | bytes 1204232 | tf_op jit(solution)/shard_map/ppermute | solution.py:474
  4.4 12.5 %collective-permute-start.1 = (bf16[784,256]{1,0:T(8,128)(2,1)S(1)}, bf16[784,256]{1,0:T(8,128)(2,1)S(1)}, u32[]{:S(2)}, u32[]{:S(2)}) collective-permute-start(bf16[784,256]{1,0:T(8,128)(2,1)S(1)} %select_kept.1.refs_0_.refs_10_), channel_id=1, source_target_pairs={{0,4},{1,5},{2,6},{3,7},{4,0},{5,1},{6,2},{7,3},{8,12},{9,13},{10,... | collective-permute-start | bytes 1204232 | tf_op jit(solution)/shard_map/ppermute | solution.py:474
  7.4 11.0 %collective-permute-start = (bf16[784,256]{1,0:T(8,128)(2,1)S(1)}, bf16[784,256]{1,0:T(8,128)(2,1)S(1)}, u32[]{:S(2)}, u32[]{:S(2)}) collective-permute-start(bf16[784,256]{1,0:T(8,128)(2,1)S(1)} %select_kept.1.refs_0_.refs_10_), channel_id=1, source_target_pairs={{0,2},{1,3},{2,0},{3,1},{4,6},{5,7},{6,4},{7,5},{8,10},{9,11},{10,... | collective-permute-start | bytes 1204232 | tf_op jit(solution)/shard_map/ppermute | solution.py:474
  18.4 8.7 %collective-permute-start.5 = (bf16[784,256]{1,0:T(8,128)(2,1)S(1)}, bf16[784,256]{1,0:T(8,128)(2,1)S(1)}, u32[]{:S(2)}, u32[]{:S(2)}) collective-permute-start(bf16[784,256]{1,0:T(8,128)(2,1)S(1)} %collective-permute-done.refs_2_.refs_12_), channel_id=1, source_target_pairs={{0,1},{1,0},{2,3},{3,2},{4,5},{5,4},{6,7},{7,6},{8,9},{9,8},{10,11... | collective-permute-start | bytes 1204232 | tf_op jit(solution)/shard_map/ppermute | solution.py:474
  18.4 8.7 %collective-permute-start.6 = (bf16[784,256]{1,0:T(8,128)(2,1)S(1)}, bf16[784,256]{1,0:T(8,128)(2,1)S(1)}, u32[]{:S(2)}, u32[]{:S(2)}) collective-permute-start(bf16[784,256]{1,0:T(8,128)(2,1)S(1)} %collective-permute-done.1.refs_4_.refs_14_), channel_id=1, source_target_pairs={{0,1},{1,0},{2,3},{3,2},{4,5},{5,4},{6,7},{7,6},{8,9},{9,8},{10,11... | collective-permute-start | bytes 1204232 | tf_op jit(solution)/shard_map/ppermute | solution.py:474
  18.9 30.5 %copy-start.1 = (bf16[256,4096]{1,0:T(8,128)(2,1)S(1)}, bf16[256,4096]{1,0:T(8,128)(2,1)}, u32[]{:S(2)}) copy-start(bf16[256,4096]{1,0:T(8,128)(2,1)} %tokens_ref.1) | copy-start | bytes 6291460
  18.9 7.0 %collective-permute-start.4 = (bf16[784,128]{1,0:T(8,128)(2,1)S(1)}, bf16[784,128]{1,0:T(8,128)(2,1)S(1)}, u32[]{:S(2)}, u32[]{:S(2)}) collective-permute-start(bf16[784,128]{1,0:T(8,128)(2,1)S(1)} %slice.19), channel_id=1, source_target_pairs={{0,2},{1,3},{2,0},{3,1},{4,6},{5,7},{6,4},{7,5},{8,10},{9,11},{10,... | collective-permute-start | bytes 602120 | tf_op jit(solution)/shard_map/ppermute | solution.py:474
  20.5 6.6 %collective-permute-start.3 = (bf16[784,128]{1,0:T(8,128)(2,1)S(1)}, bf16[784,128]{1,0:T(8,128)(2,1)S(1)}, u32[]{:S(2)}, u32[]{:S(2)}) collective-permute-start(bf16[784,128]{1,0:T(8,128)(2,1)S(1)} %slice.18), channel_id=1, source_target_pairs={{0,4},{1,5},{2,6},{3,7},{4,0},{5,1},{6,2},{7,3},{8,12},{9,13},{10,... | collective-permute-start | bytes 602120 | tf_op jit(solution)/shard_map/ppermute | solution.py:474
  27.1 3.6 %collective-permute-start.7 = (bf16[784,128]{1,0:T(8,128)(2,1)S(1)}, bf16[784,128]{1,0:T(8,128)(2,1)S(1)}, u32[]{:S(2)}, u32[]{:S(2)}) collective-permute-start(bf16[784,128]{1,0:T(8,128)(2,1)S(1)} %collective-permute-done.3.refs_6_.refs_16_), channel_id=1, source_target_pairs={{0,1},{1,0},{2,3},{3,2},{4,5},{5,4},{6,7},{7,6},{8,9},{9,8},{10,11... | collective-permute-start | bytes 602120 | tf_op jit(solution)/shard_map/ppermute | solution.py:474
  27.1 22.1 %collective-permute-start.11 = (bf16[32,4096]{1,0:T(8,128)(2,1)S(1)}, bf16[32,4096]{1,0:T(8,128)(2,1)S(1)}, u32[]{:S(2)}, u32[]{:S(2)}) collective-permute-start(bf16[32,4096]{1,0:T(8,128)(2,1)S(1)} %copy-done.3), channel_id=1, source_target_pairs={{0,6},{1,7},{2,4},{3,5},{4,2},{5,3},{6,0},{7,1},{8,14},{9,15},{10,... | collective-permute-start | bytes 786440 | tf_op jit(solution)/shard_map/ppermute | solution.py:474
  27.6 21.7 %collective-permute-start.10 = (bf16[32,4096]{1,0:T(8,128)(2,1)S(1)}, bf16[32,4096]{1,0:T(8,128)(2,1)S(1)}, u32[]{:S(2)}, u32[]{:S(2)}) collective-permute-start(bf16[32,4096]{1,0:T(8,128)(2,1)S(1)} %copy-done.3), channel_id=1, source_target_pairs={{0,4},{1,5},{2,6},{3,7},{4,0},{5,1},{6,2},{7,3},{8,12},{9,13},{10,... | collective-permute-start | bytes 786440 | tf_op jit(solution)/shard_map/ppermute | solution.py:474
  29.2 20.0 %collective-permute-start.9 = (bf16[32,4096]{1,0:T(8,128)(2,1)S(1)}, bf16[32,4096]{1,0:T(8,128)(2,1)S(1)}, u32[]{:S(2)}, u32[]{:S(2)}) collective-permute-start(bf16[32,4096]{1,0:T(8,128)(2,1)S(1)} %copy-done.3), channel_id=1, source_target_pairs={{0,2},{1,3},{2,0},{3,1},{4,6},{5,7},{6,4},{7,5},{8,10},{9,11},{10,... | collective-permute-start | bytes 786440 | tf_op jit(solution)/shard_map/ppermute | solution.py:474
  30.7 1.4 %collective-permute-start.8 = (bf16[784,128]{1,0:T(8,128)(2,1)S(1)}, bf16[784,128]{1,0:T(8,128)(2,1)S(1)}, u32[]{:S(2)}, u32[]{:S(2)}) collective-permute-start(bf16[784,128]{1,0:T(8,128)(2,1)S(1)} %collective-permute-done.4.refs_7_.refs_17_), channel_id=1, source_target_pairs={{0,1},{1,0},{2,3},{3,2},{4,5},{5,4},{6,7},{7,6},{8,9},{9,8},{10,11... | collective-permute-start | bytes 602120 | tf_op jit(solution)/shard_map/ppermute | solution.py:474
  51.2 5.8 %collective-permute-start.15 = (f32[32,512]{1,0:T(8,128)S(1)}, f32[32,512]{1,0:T(8,128)S(1)}, u32[]{:S(2)}, u32[]{:S(2)}) collective-permute-start(f32[32,512]{1,0:T(8,128)S(1)} %get-tuple-element.43), channel_id=1, source_target_pairs={{0,6},{1,7},{2,4},{3,5},{4,2},{5,3},{6,0},{7,1},{8,14},{9,15},{10,... | collective-permute-start | bytes 196616 | tf_op jit(solution)/shard_map/ppermute | solution.py:474
  51.6 5.4 %collective-permute-start.14 = (f32[32,512]{1,0:T(8,128)S(1)}, f32[32,512]{1,0:T(8,128)S(1)}, u32[]{:S(2)}, u32[]{:S(2)}) collective-permute-start(f32[32,512]{1,0:T(8,128)S(1)} %get-tuple-element.44), channel_id=1, source_target_pairs={{0,4},{1,5},{2,6},{3,7},{4,0},{5,1},{6,2},{7,3},{8,12},{9,13},{10,... | collective-permute-start | bytes 196616 | tf_op jit(solution)/shard_map/ppermute | solution.py:474
  53.2 4.3 %collective-permute-start.13 = (f32[32,512]{1,0:T(8,128)S(1)}, f32[32,512]{1,0:T(8,128)S(1)}, u32[]{:S(2)}, u32[]{:S(2)}) collective-permute-start(f32[32,512]{1,0:T(8,128)S(1)} %get-tuple-element.45), channel_id=1, source_target_pairs={{0,2},{1,3},{2,0},{3,1},{4,6},{5,7},{6,4},{7,5},{8,10},{9,11},{10,... | collective-permute-start | bytes 196616 | tf_op jit(solution)/shard_map/ppermute | solution.py:474
where the time goes:
time: 74.7 us; the launch traced here: 74.6 us
  Pallas kernels  35.6 us (48%)
  waiting for transfers between devices  19.8 us (27%)
  starting transfers between devices  14.7 us (20%)
  local copies, waits for them, and re-layouts  2.38 us (3%)
  matrix products  1.71 us (2%)
    ppermute x16, waiting for transfers between devices, swap(): return lax.ppermute(x, 'dp', [(d, d ^ k) for d in range(n)])  19.8 us
    pallas_call x1, Pallas kernels, first_half(): pl.pallas_call(body, out_shape=[jax.ShapeDtypeStruct((kept, kept), jnp.fl...  17.1 us
    pallas_call x1, Pallas kernels, second_half(): pl.pallas_call(body, out_shape=jax.ShapeDtypeStruct((own, features), jnp....  16.9 us
    ppermute x16, starting transfers between devices, swap(): return lax.ppermute(x, 'dp', [(d, d ^ k) for d in range(n)])  14.7 us
    unnamed x11, local copies, waits for them, and re-layouts  2.31 us
    dot_general x2, matrix products, on_device(): lax.dot_general(stacked, part, NT, preferred_element_type=jnp.float32)  1.71 us
    pallas_call x1, Pallas kernels, select_kept(): pl.pallas_call(select_kernel, out_shape=jax.ShapeDtypeStruct((kept + EXTR...  1.58 us
  transfers between devices with their start and end apart: 16, of which 7 were waited for; matrix products, arithmetic and copies ran while one was open for 0% of the time, Pallas kernels for 25%

commit v1 on v0

--- a/solution.py
+++ b/solution.py
@@ -12,6 +12,7 @@
 SUB = 8
 EXTRA = 16
 VMEM_LIMIT = 32 * 1024 * 1024
+VMEM_LARGE = 60 * 1024 * 1024
 NT = (((1,), (1,)), ((), ()))
 NN = (((1,), (0,)), ((), ()))
 
@@ -92,7 +93,7 @@
             pltpu.VMEM((rows, features), jnp.bfloat16),
             pltpu.SemaphoreType.DMA((chunks,)),
         ],
-        compiler_params=pltpu.CompilerParams(vmem_limit_bytes=VMEM_LIMIT),
+        compiler_params=pltpu.CompilerParams(vmem_limit_bytes=VMEM_LARGE),
         name="select_kept",
     )(keep_flags, tokens)
 
@@ -123,62 +124,50 @@
 
 def solve_small(entry, rows, cross, ahead):
     entry, rows, cross, ahead = dict(entry), list(rows), list(cross), list(ahead)
-    inverse = {}
-    following = {}
+    lower = {}
     for t in range(0, SUB, 2):
         u = t + 1
         a, b, c = entry[t, t], entry[t, u], entry[u, u]
         first = pl.reciprocal(a, approx=True)
         second = a * pl.reciprocal(a * c - b * b, approx=True)
-        step = b * first
+        lower[u, t] = b * first
         later = range(u + 1, SUB)
-        one = {j: entry[t, j] * first for j in later}
-        rest = {j: entry[u, j] - b * one[j] for j in later}
+        rest = {}
+        for j in later:
+            lower[j, t] = entry[t, j] * first
+            rest[j] = entry[u, j] - b * lower[j, t]
         for j in later:
             for i in range(u + 1, j + 1):
-                partial = entry[i, j] - entry[t, i] * one[j]
+                partial = entry[i, j] - entry[t, i] * lower[j, t]
                 entry[i, j] = partial - (rest[i] * rest[j]) * second
-        two = {j: rest[j] * second for j in later}
+        for j in later:
+            lower[j, u] = rest[j] * second
+        for part in (cross, rows):
+            if part:
+                part[u] = part[u] - lower[u, t] * part[t]
+                for j in later:
+                    part[j] = (part[j] - lower[j, t] * part[t]) - lower[j, u] * part[u]
         if cross:
-            cross[u] = cross[u] - step * cross[t]
-            for j in later:
-                cross[j] = (cross[j] - one[j] * cross[t]) - two[j] * cross[u]
-            if u + 1 < SUB:
-                left, right = cross[t] * first, cross[u] * second
-                for j in range(SUB):
-                    ahead[j] = (ahead[j] - left * sublane_row(cross[t], j)) - right * sublane_row(cross[u], j)
-            else:
-                left = [sublane_row(cross[t], j) for j in range(SUB)]
-                right = [sublane_row(cross[u], j) for j in range(SUB)]
-                for j in range(SUB):
-                    for i in range(j + 1):
-                        value = sublane_row(ahead[j], i) - (left[i] * left[j]) * first
-                        following[i, j] = value - (right[i] * right[j]) * second
-        rows[u] = rows[u] - step * rows[t]
-        inverse[u, t] = -step
-        for k in range(t):
-            inverse[u, k] = inverse[u, k] - step * inverse[t, k]
-        for j in later:
-            rows[j] = (rows[j] - one[j] * rows[t]) - two[j] * rows[u]
-            for k in range(t):
-                inverse[j, k] = (inverse[j, k] - one[j] * inverse[t, k]) - two[j] * inverse[u, k]
-            inverse[j, t] = -one[j] - two[j] * inverse[u, t]
-            inverse[j, u] = -two[j]
+            left, right = cross[t] * first, cross[u] * second
+            for j in range(SUB):
+                ahead[j] = (ahead[j] - left * sublane_row(cross[t], j)) - right * sublane_row(cross[u], j)
         rows[t] = rows[t] * first
         rows[u] = rows[u] * second
-    rows = [
-        tree_sum([rows[i]] + [inverse[j, i] * rows[j] for j in range(i + 1, SUB)]) for i in range(SUB)
-    ]
+    following = {(i, j): sublane_row(ahead[j], i) for j in range(SUB) for i in range(j + 1) if cross}
+    for t in reversed(range(SUB)):
+        for j in range(t):
+            rows[j] = rows[j] - lower[t, j] * rows[t]
     return rows, following
 
 
-def invert_panel(block, beside=()):
+def factor_panel(block, beside=()):
     size = block.shape[0]
     count = size // SUB
     sub = lax.broadcasted_iota(jnp.int32, (SUB, 128), 0)
     lane = lax.broadcasted_iota(jnp.int32, (SUB, 128), 1)
     rows = [block[i * SUB:(i + 1) * SUB, :] for i in range(count)]
     entry = block_entries(rows[0], 0)
+    lower, scaled = [], []
     done = 0
     for s in range(count):
         base = s * SUB
@@ -189,19 +178,20 @@
             ahead = [lane_column(rows[s + 1], base + SUB + j) for j in range(SUB)]
         pivot_rows = jnp.where(inside, jnp.where(lane == sub + base, 1.0, 0.0), rows[s])
         spread, entry = solve_small(entry, [sublane_row(pivot_rows, j) for j in range(SUB)], cross, ahead)
-        for i in [(s + d) % count for d in range(1, count)]:
+        for i in range(s + 1, count):
             columns = cross if i == s + 1 else [lane_column(rows[i], base + j) for j in range(SUB)]
             change = tree_sum([columns[j] * spread[j] for j in range(SUB)])
             rows[i] = jnp.where(inside, 0.0, rows[i]) - change
         new = spread[SUB - 1]
         for j in range(SUB - 1):
             new = jnp.where(sub == j, spread[j], new)
-        rows[s] = new
+        lower.append(jnp.where(lane < base + SUB, pivot_rows, 0.0))
+        scaled.append(jnp.where(lane < base + SUB, new, 0.0))
         until = len(beside) * (s + 1) // count
         for task in beside[done:until]:
             task()
         done = until
-    return jnp.concatenate(rows, axis=0)
+    return jnp.concatenate(lower, axis=0), jnp.concatenate(scaled, axis=0)
 
 
 def wide_left(x):
@@ -212,6 +202,11 @@
 def wide_right(x):
     hi, mid, low = split3(x)
     return jnp.concatenate([hi, mid, hi, low, mid, hi], axis=0)
+
+
+def wide_across(x):
+    hi, mid, low = split3(x)
+    return jnp.concatenate([hi, mid, hi, low, mid, hi], axis=1)
 
 
 def spans(low, high):
@@ -220,40 +215,56 @@
     return list(zip(starts, starts[1:] + [high]))
 
 
-def settle_tasks(p, state):
-    a_ref, wide_ref, _, w_ref, left_ref, right_ref = state
-    kept = a_ref.shape[0]
+def settle_tasks(p, state, lower_ref, scaled_ref):
+    a_ref, offset, _, w_ref, left_ref, right_ref = state
+    kept = w_ref.shape[1]
     at = p * PANEL
     low = at + PANEL
-    here = slice(at, low)
+    here = slice(at - offset, low - offset)
+    rest = slice(low - offset, kept - offset)
 
     def make_w(c, d):
-        value = dot32(wide_ref[...], wide_right(a_ref[here, c:d]), NN)
-        w_ref[:, c:d] = value
+        value = dot32(wide_left(scaled_ref[...]), wide_right(a_ref[here, c - offset:d - offset]), NN)
         right_ref[:, c:d] = wide_right(value)
 
     def make_left():
-        left_ref[low:, :] = wide_left(a_ref[low:, here])
+        value = dot32(wide_left(a_ref[rest, here]), wide_across(lower_ref[...]), NT)
+        left_ref[low:, :] = wide_left(value)
 
     def update(c, d):
-        a_ref[low:, c:d] -= dot32(left_ref[low:, :], right_ref[:, c:d], NN)
-
-    def place():
-        a_ref[here, low:] = w_ref[:, low:]
-
-    tasks = [functools.partial(make_w, c, d) for c, d in spans(low, kept)] + [make_left]
-    return tasks + [functools.partial(update, c, d) for c, d in spans(low, kept)] + [place]
-
-
-def panel(p, state, pivot_ref, beside):
-    a_ref, wide_ref, next_ref = state[:3]
-    here, after = slice(p * PANEL, (p + 1) * PANEL), slice((p + 1) * PANEL, (p + 2) * PANEL)
-    inverse = invert_panel(next_ref[...], beside)
-    wide = wide_left(inverse)
-    crossing = dot32(wide, wide_right(a_ref[here, after]), NN)
-    next_ref[...] = a_ref[after, after] - dot32(wide_left(a_ref[after, here]), wide_right(crossing), NN)
-    pivot_ref[...] = inverse
-    wide_ref[...] = wide
+        a_ref[rest, c - offset:d - offset] -= dot32(left_ref[low:, :], right_ref[:, c:d], NN)
+
+    def place(c, d):
+        a_ref[here, c - offset:d - offset] = dot32(wide_left(lower_ref[...].T), right_ref[:, c:d], NN)
+
+    ranges = spans(low, kept)
+    tasks = [functools.partial(make_w, c, d) for c, d in ranges] + [make_left]
+    tasks += [functools.partial(update, c, d) for c, d in ranges]
+    return tasks + [functools.partial(place, c, d) for c, d in ranges]
+
+
+def panel(p, state, factors_ref, beside):
+    a_ref, offset, next_ref = state[:3]
+    at = p * PANEL - offset
+    here, after = slice(at, at + PANEL), slice(at + PANEL, at + 2 * PANEL)
+    lower, scaled = factor_panel(next_ref[...], beside)
+    left = dot32(wide_left(a_ref[after, here]), wide_across(lower), NT)
+    right = dot32(wide_left(scaled), wide_right(a_ref[here, after]), NN)
+    next_ref[...] = a_ref[after, after] - dot32(wide_left(left), wide_right(right), NN)
+    factors_ref[0] = lower
+    factors_ref[1] = scaled
+
+
+def factors_shape(count):
+    return jax.ShapeDtypeStruct((count, 2, PANEL, PANEL), jnp.float32)
+
+
+def work_scratch(kept):
+    return [
+        pltpu.VMEM((8, kept), jnp.float32),
+        pltpu.VMEM((kept, 6 * PANEL), jnp.bfloat16),
+        pltpu.VMEM((6 * PANEL, kept), jnp.bfloat16),
+    ]
 
 
 def place_pieces(pieces, all_ref, sem):
@@ -268,8 +279,7 @@
 
 
 def first_kernel(features, rows, last, *refs):
-    pieces, refs = refs[:-9], refs[-9:]
-    a_ref, scale_ref, pivot_ref, wide_ref, next_ref, all_ref, w_ref, left_ref, right_ref = refs
+    a_ref, scale_ref, factors_ref, next_ref, all_ref, w_ref, left_ref, right_ref = refs[-8:]
     kept = a_ref.shape[0]
     tokens = all_ref.shape[1]
     total = jnp.float32(0.0)
@@ -290,13 +300,13 @@
 
     gram(0, 256)
     next_ref[...] = a_ref[:PANEL, :PANEL]
-    state = (a_ref, wide_ref, next_ref, w_ref, left_ref, right_ref)
+    state = (a_ref, 0, next_ref, w_ref, left_ref, right_ref)
     for p in range(last):
         if p:
-            tasks = settle_tasks(p - 1, state)
+            tasks = settle_tasks(p - 1, state, factors_ref.at[p - 1, 0], factors_ref.at[p - 1, 1])
         else:
             tasks = [functools.partial(gram, at, 256) for at in range(256, kept, 256)]
-        panel(p, state, pivot_ref.at[p], tasks)
+        panel(p, state, factors_ref.at[p], tasks)
 
 
 def first_half(pieces, features, last):
@@ -307,7 +317,7 @@
 
     def body(*refs):
         refs, sem = refs[:-1], refs[-1]
-        for copy in place_pieces(refs[:count], refs[count + 5], sem):
+        for copy in place_pieces(refs[:count], refs[count + 4], sem):
             copy.wait()
         first_kernel(float(features), rows, last, *refs)
 
@@ -316,17 +326,14 @@
         out_shape=[
             jax.ShapeDtypeStruct((kept, kept), jnp.float32),
             jax.ShapeDtypeStruct((8, 128), jnp.float32),
-            jax.ShapeDtypeStruct((last, PANEL, PANEL), jnp.float32),
-            jax.ShapeDtypeStruct((PANEL, 6 * PANEL), jnp.bfloat16),
+            factors_shape(last),
             jax.ShapeDtypeStruct((PANEL, PANEL), jnp.float32),
         ],
         in_specs=[pl.BlockSpec(memory_space=pl.ANY)] * count,
-        out_specs=[pl.BlockSpec(memory_space=pltpu.VMEM)] * 5,
+        out_specs=[pl.BlockSpec(memory_space=pltpu.VMEM)] * 4,
         scratch_shapes=[
             pltpu.VMEM((kept_extra, tokens), jnp.bfloat16),
-            pltpu.VMEM((PANEL, kept), jnp.float32),
-            pltpu.VMEM((kept, 6 * PANEL), jnp.bfloat16),
-            pltpu.VMEM((6 * PANEL, kept), jnp.bfloat16),
+            *work_scratch(kept),
             pltpu.SemaphoreType.DMA((count,)),
         ],
         compiler_params=pltpu.CompilerParams(vmem_limit_bytes=VMEM_LIMIT),
@@ -345,35 +352,73 @@
     return small + (first[rows:2 * rows] + second[:rows]) + first[:rows]
 
 
-def second_kernel(chips, first, copies, flags_ref, *refs):
+def middle_kernel(first, last, start_ref, early_ref, start_next_ref, a_ref, factors_ref, next_ref, *work):
+    kept = start_ref.shape[0]
+    offset = kept - a_ref.shape[0]
+    a_ref[...] = start_ref[offset:, offset:]
+    next_ref[...] = start_next_ref[...]
+    state = (a_ref, offset, next_ref, *work)
+    for p in range(first, last):
+        source = early_ref.at[p - 1] if p == first else factors_ref.at[p - 1 - first]
+        panel(p, state, factors_ref.at[p - first], settle_tasks(p - 1, state, source.at[0], source.at[1]))
+
+
+def middle_part(a, factors, follow, first, last):
+    kept = a.shape[0]
+    left = kept - (first - 1) * PANEL
+    vmem = pl.BlockSpec(memory_space=pltpu.VMEM)
+    return pl.pallas_call(
+        functools.partial(middle_kernel, first, last),
+        out_shape=[
+            jax.ShapeDtypeStruct((left, left), jnp.float32),
+            factors_shape(last - first),
+            jax.ShapeDtypeStruct((PANEL, PANEL), jnp.float32),
+        ],
+        in_specs=[vmem] * 3,
+        out_specs=[vmem] * 3,
+        scratch_shapes=work_scratch(kept),
+        compiler_params=pltpu.CompilerParams(vmem_limit_bytes=VMEM_LIMIT),
+        name="middle_panels",
+    )(a, factors, follow)
+
+
+def last_kernel(chips, begin, middle, copies, flags_ref, *refs):
     projected, refs = refs[:chips], refs[chips:]
-    start_ref, early_ref, start_wide_ref, start_next_ref, scale_ref = refs[:5]
-    out_ref, index_ref, wide_out_ref, all_ref, late_ref = refs[-11:-6]
-    state = refs[-6:]
-    a_ref, wide_ref, next_ref = state[:3]
+    scale_ref, whole_ref, early_ref, start_ref, mid_ref, start_next_ref = refs[:6]
+    out_ref, index_ref, wide_out_ref, all_ref, late_ref, a_ref, next_ref = refs[-10:-3]
+    work = refs[-3:]
     own, features = out_ref.shape
     blocks = flags_ref.shape[0]
     width = features // blocks
     per_tile = 128 // width
-    kept = a_ref.shape[0]
+    kept = whole_ref.shape[0]
     last = kept // PANEL - 1
     at = last * PANEL
     kept_blocks(flags_ref, index_ref)
     wide_out_ref[...] = jnp.zeros((own, features), jnp.float32)
-    live = (first - 1) * PANEL
-    a_ref[live:, live:] = start_ref[live:, live:]
-    wide_ref[...] = start_wide_ref[...]
+    offset = kept - a_ref.shape[0]
+    cut = start_ref.shape[0] - a_ref.shape[0]
+    a_ref[...] = start_ref[cut:, cut:]
     next_ref[...] = start_next_ref[...]
+    state = (a_ref, offset, next_ref, *work)
     held = {}
 
-    def block(p):
-        return slice(p * PANEL, (p + 1) * PANEL)
-
     def factor(p):
-        return (start_ref if p < first - 1 else a_ref)[block(p), (p + 1) * PANEL:]
-
-    def pivot(p):
-        return early_ref[p] if p < first else late_ref[p - first]
+        source, skip = a_ref, offset
+        if p < begin - 1:
+            source, skip = whole_ref, 0
+        elif p < middle - 1:
+            source, skip = start_ref, kept - start_ref.shape[0]
+        low = p * PANEL - skip
+        return source[low:low + PANEL, low + PANEL:]
+
+    def factors(p):
+        if p < begin:
+            return early_ref.at[p]
+        return mid_ref.at[p - begin] if p < middle else late_ref.at[p - middle]
+
+    def settle(p):
+        return settle_tasks(p, state, factors(p).at[0], factors(p).at[1])
 
     def make_right():
         whole = jnp.concatenate([part[...] for part in projected], axis=1)
@@ -386,7 +431,7 @@
         held["right"] = right[:, PANEL:] - dot_small(right[:, :PANEL], factor(p))
 
     def scaled(p):
-        held["zd", p] = dot_small(held["z", p], pivot(p))
+        held["zd", p] = dot_small(dot_small(held["z", p], factors(p)[0], NT), factors(p)[1])
 
     def backward(p):
         if p == last:
@@ -398,19 +443,19 @@
             value = base - dot_small(held["back"], factor(p), NT)
             held["back"] = jnp.concatenate([value, held["back"]], axis=1)
 
-    for p in range(first, last):
-        tasks = settle_tasks(p - 1, state)
+    for copy in copies:
+        copy.wait()
+    for p in range(middle, last):
+        tasks = settle(p - 1)
         if p == last - 1:
-            for copy in copies:
-                copy.wait()
             tasks = [make_right] + [functools.partial(forward, q) for q in range(p - 1)] + tasks
             tasks += [functools.partial(forward, p - 1)] + [functools.partial(scaled, q) for q in range(p)]
-        panel(p, state, late_ref.at[p - first], tasks)
-    tasks = settle_tasks(last - 1, state)
+        panel(p, state, late_ref.at[p - middle], tasks)
+    tasks = settle(last - 1)
     tasks += [functools.partial(forward, last - 1), functools.partial(scaled, last - 1)]
     tasks += [functools.partial(backward, p) for p in reversed(range(last + 1))]
-    inverse = invert_panel(next_ref[...], tasks)
-    tail = dot_small(held["right"], inverse)
+    lower, upper = factor_panel(next_ref[...], tasks)
+    tail = dot_small(dot_small(held["right"], lower, NT), upper)
     scale = scale_ref[0:1, 0:1]
     front = held["back"][:own, :at] + dot_small(tail, held["back"][own:, :at])
     answer = [front[:, c:c + PANEL] * scale for c in range(0, at, PANEL)] + [tail * scale]
@@ -427,43 +472,41 @@
     out_ref[...] = wide_out_ref[...].astype(jnp.bfloat16)
 
 
-def second_half(keep_flags, projected, begun, scale, pieces, features, first):
+def last_part(keep_flags, projected, begun, pieces, features, begin, middle):
     own = projected[0].shape[0]
     blocks = keep_flags.shape[0]
     chips = len(projected)
-    kept = begun[0].shape[0]
+    kept = begun[1].shape[0]
     count = len(pieces)
     tokens = sum(piece.shape[1] for piece in pieces)
+    left = kept - (middle - 1) * PANEL
     vmem = pl.BlockSpec(memory_space=pltpu.VMEM)
     anywhere = pl.BlockSpec(memory_space=pl.ANY)
 
     def body(*refs):
         refs, sem = refs[:-1], refs[-1]
-        ins = 6 + chips
+        ins = 1 + chips + len(begun)
         copies = place_pieces(refs[ins:ins + count], refs[ins + count + 3], sem)
-        second_kernel(chips, first, copies, *refs)
+        last_kernel(chips, begin, middle, copies, *refs)
 
     return pl.pallas_call(
         body,
         out_shape=jax.ShapeDtypeStruct((own, features), jnp.bfloat16),
-        in_specs=[pl.BlockSpec(memory_space=pltpu.SMEM)] + [vmem] * (chips + 5) + [anywhere] * count,
+        in_specs=[pl.BlockSpec(memory_space=pltpu.SMEM)] + [vmem] * (chips + len(begun)) + [anywhere] * count,
         out_specs=vmem,
         scratch_shapes=[
             pltpu.SMEM((blocks + 1,), jnp.int32),
             pltpu.VMEM((own, features), jnp.float32),
             pltpu.VMEM((kept + EXTRA, tokens), jnp.bfloat16),
-            pltpu.VMEM((kept // PANEL - 1 - first, PANEL, PANEL), jnp.float32),
-            pltpu.VMEM((kept, kept), jnp.float32),
-            pltpu.VMEM((PANEL, 6 * PANEL), jnp.bfloat16),
+            pltpu.VMEM((kept // PANEL - 1 - middle, 2, PANEL, PANEL), jnp.float32),
+            pltpu.VMEM((left, left), jnp.float32),
             pltpu.VMEM((PANEL, PANEL), jnp.float32),
-            pltpu.VMEM((PANEL, kept), jnp.float32),
-            pltpu.VMEM((kept, 6 * PANEL), jnp.bfloat16),
-            pltpu.VMEM((6 * PANEL, kept), jnp.bfloat16),
+            *work_scratch(kept),
             pltpu.SemaphoreType.DMA((count,)),
         ],
         compiler_params=pltpu.CompilerParams(vmem_limit_bytes=VMEM_LIMIT),
         name="last_panels_and_solution",
-    )(keep_flags, *projected, *begun, scale, *pieces)
+    )(keep_flags, *projected, *begun, *pieces)
 
 
 def solution(mesh):
@@ -492,21 +535,25 @@
         own = orig_weight.shape[0]
         kept = select_kept(tokens, keep_flags)
         panels = (kept.shape[0] - EXTRA) // PANEL
-        half = panels // 2
+        begin = panels // 2
+        middle = begin + 1
+        tokens, kept = lax.optimization_barrier((tokens, kept))
         pieces, arrived = gather_kept(kept)
         orig_weight, arrived = lax.optimization_barrier((orig_weight, arrived))
         sibling = swap(tokens, 1)
         weights = [orig_weight] + [swap(orig_weight, k) for k in others]
-        a, scale, *state = first_half(pieces, features, half)
+        a, scale, factors, follow = first_half(pieces, features, begin)
         a, weights, sibling = lax.optimization_barrier((a, weights, sibling))
         stacked = jnp.concatenate(weights, axis=0)
         projected = [
             lax.dot_general(stacked, part, NT, preferred_element_type=jnp.float32) for part in (tokens, sibling)
         ]
-        projected = lax.optimization_barrier(jnp.concatenate(projected, axis=1))
+        projected, a = lax.optimization_barrier((jnp.concatenate(projected, axis=1), a))
         parts = [projected[i * own:(i + 1) * own] for i in range(n // 2)]
         parts = [parts[0]] + [swap(part, k) for part, k in zip(parts[1:], others)]
-        return second_half(keep_flags, parts, (a, *state), scale, pieces, features, half)
+        rest, more, follow = middle_part(a, factors, follow, begin, middle)
+        begun = (scale, a, factors, rest, more, follow)
+        return last_part(keep_flags, parts, begun, pieces, features, begin, middle)
 
     in_specs = (P("dp", None), P(("section", "dp"), None), P())
     out_specs = P(("section", "dp"), None)

time: 74.7 us -> 66.5 us (0.89)
  Pallas kernels: 35.6 us -> 30.9 us
  waiting for transfers between devices: 19.8 us -> 17.3 us
  local copies, waits for them, and re-layouts: 2.38 us -> 1.14 us
    pallas_call x1, Pallas kernels: 17.1 us -> 13.1 us  [first_half(): pl.pallas_call(body, out_shape=[jax.ShapeDtypeStruct((kept, kept), jnp.fl...]
    pallas_call x1 -> x2, Pallas kernels: 16.9 us -> 14 us  [the longest x1 10.1 us: last_part(): pl.pallas_call(body, out_shape=jax.ShapeDtypeStruct((own, features), jnp....]
    ppermute x16, waiting for transfers between devices: 19.8 us -> 17.3 us  [swap(): return lax.ppermute(x, 'dp', [(d, d ^ k) for d in range(n)])]
    pallas_call x1, Pallas kernels: 1.58 us -> 3.85 us  [select_kept(): pl.pallas_call(select_kernel, out_shape=jax.ShapeDtypeStruct((kept + EXTR...]
    unnamed x11 -> x13, local copies, waits for them, and re-layouts: 2.31 us -> 1.07 us
  transfers between devices with their start and end apart: 16 -> 16, of which waited for: 7 -> 5; matrix products, arithmetic and copies ran while one was open for 0% -> 0% of each run, Pallas kernels for 25% -> 26%
where the time goes in v1:
time: 66.5 us; the launch traced here: 66.3 us
  Pallas kernels  30.9 us (46%)
  waiting for transfers between devices  17.3 us (26%)
  starting transfers between devices  14.7 us (22%)
  matrix products  1.84 us (3%)
  local copies, waits for them, and re-layouts  1.14 us (2%)
    ppermute x16, waiting for transfers between devices, swap(): return lax.ppermute(x, 'dp', [(d, d ^ k) for d in range(n)])  17.3 us
    ppermute x16, starting transfers between devices, swap(): return lax.ppermute(x, 'dp', [(d, d ^ k) for d in range(n)])  14.7 us
    pallas_call x1, Pallas kernels, first_half(): pl.pallas_call(body, out_shape=[jax.ShapeDtypeStruct((kept, kept), jnp.fl...  13.1 us
    pallas_call x1, Pallas kernels, last_part(): pl.pallas_call(body, out_shape=jax.ShapeDtypeStruct((own, features), jnp....  10.1 us
    pallas_call x1, Pallas kernels, middle_part(): pl.pallas_call(functools.partial(middle_kernel, first, last), out_shape=[...  3.9 us
    pallas_call x1, Pallas kernels, select_kept(): pl.pallas_call(select_kernel, out_shape=jax.ShapeDtypeStruct((kept + EXTR...  3.85 us
    dot_general x2, matrix products, on_device(): lax.dot_general(stacked, part, NT, preferred_element_type=jnp.float32)  1.84 us
  transfers between devices with their start and end apart: 16, of which 5 were waited for; matrix products, arithmetic and copies ran while one was open for 0% of the time, Pallas kernels for 26%

profile of v1, /device:TPU:0, one launch (start us, length us, event | category | flops | bytes accessed | tf_op | source)
XLA Modules:
  0.0 66.3 jit_solution(10670998981871497878)
XLA Ops:
  0.0 0.0 copy-start.3
  0.0 0.0 copy-start.4
  0.0 3.9 %select_kept.1.refs_0_.refs_11_ = bf16[784,256]{1,0:T(8,128)(2,1)} custom-call(s32[64]{0:T(128)} %refs_0_.1, bf16[256,4096]{1,0:T(8,128)(2,1)} %tokens_ref.1), custom_call_target="tpu_custom_call" | custom-call | tf_op jit(solution)/shard_map/select_kept/pallas_call | solution.py:83
  3.9 0.0 copy-done.3
  3.9 0.5 collective-permute-start.12
  4.4 0.1 collective-permute-start.2
  4.5 2.9 %collective-permute-start.1 = (bf16[784,256]{1,0:T(8,128)(2,1)}, bf16[784,256]{1,0:T(8,128)(2,1)S(1)}, u32[]{:S(2)}, u32[]{:S(2)}) collective-permute-start(bf16[784,256]{1,0:T(8,128)(2,1)} %select_kept.1.refs_0_.refs_11_), channel_id=1, source_target_pairs={{0,4},{1,5},{2,6},{3,7},{4,0},{5,1},{6,2},{7,3},{8,12},{9,13},{10,... | collective-permute-start | bytes 1204232 | tf_op jit(solution)/shard_map/ppermute | solution.py:517
  7.4 1.5 %collective-permute-start = (bf16[784,256]{1,0:T(8,128)(2,1)}, bf16[784,256]{1,0:T(8,128)(2,1)S(1)}, u32[]{:S(2)}, u32[]{:S(2)}) collective-permute-start(bf16[784,256]{1,0:T(8,128)(2,1)} %select_kept.1.refs_0_.refs_11_), channel_id=1, source_target_pairs={{0,2},{1,3},{2,0},{3,1},{4,6},{5,7},{6,4},{7,5},{8,10},{9,11},{10,... | collective-permute-start | bytes 1204232 | tf_op jit(solution)/shard_map/ppermute | solution.py:517
  8.9 0.0 collective-permute-done.2.refs_1_.refs_12_
  8.9 8.2 %collective-permute-done.1.refs_4_.refs_15_ = bf16[784,256]{1,0:T(8,128)(2,1)S(1)} collective-permute-done((bf16[784,256]{1,0:T(8,128)(2,1)}, bf16[784,256]{1,0:T(8,128)(2,1)S(1)}, u32[]{:S(2)}, u32[]{:S(2)}) %collective-permute-start.1) | collective-permute-done | bytes 401440 | tf_op jit(solution)/shard_map/ppermute | solution.py:517
  17.2 1.5 %collective-permute-done.refs_2_.refs_13_ = bf16[784,256]{1,0:T(8,128)(2,1)S(1)} collective-permute-done((bf16[784,256]{1,0:T(8,128)(2,1)}, bf16[784,256]{1,0:T(8,128)(2,1)S(1)}, u32[]{:S(2)}, u32[]{:S(2)}) %collective-permute-start) | collective-permute-done | bytes 401440 | tf_op jit(solution)/shard_map/ppermute | solution.py:517
  18.6 0.0 collective-permute-start.5
  18.6 0.5 collective-permute-start.6
  19.2 1.6 %collective-permute-start.4 = (bf16[784,128]{1,0:T(8,128)(2,1)S(1)}, bf16[784,128]{1,0:T(8,128)(2,1)S(1)}, u32[]{:S(2)}, u32[]{:S(2)}) collective-permute-start(bf16[784,128]{1,0:T(8,128)(2,1)S(1)} %slice.19), channel_id=1, source_target_pairs={{0,2},{1,3},{2,0},{3,1},{4,6},{5,7},{6,4},{7,5},{8,10},{9,11},{10,... | collective-permute-start | bytes 602120 | tf_op jit(solution)/shard_map/ppermute | solution.py:517
  20.7 0.5 collective-permute-start.3
  21.2 4.9 %collective-permute-done.4.refs_7_.refs_18_ = bf16[784,128]{1,0:T(8,128)(2,1)S(1)} collective-permute-done((bf16[784,128]{1,0:T(8,128)(2,1)S(1)}, bf16[784,128]{1,0:T(8,128)(2,1)S(1)}, u32[]{:S(2)}, u32[]{:S(2)}) %collective-permute-start.4) | collective-permute-done | bytes 200736 | tf_op jit(solution)/shard_map/ppermute | solution.py:517
  26.1 1.2 %collective-permute-done.3.refs_6_.refs_17_ = bf16[784,128]{1,0:T(8,128)(2,1)S(1)} collective-permute-done((bf16[784,128]{1,0:T(8,128)(2,1)S(1)}, bf16[784,128]{1,0:T(8,128)(2,1)S(1)}, u32[]{:S(2)}, u32[]{:S(2)}) %collective-permute-start.3) | collective-permute-done | bytes 200736 | tf_op jit(solution)/shard_map/ppermute | solution.py:517
  27.4 0.0 collective-permute-done.5.refs_3_.refs_14_
  27.4 0.0 collective-permute-done.6.refs_5_.refs_16_
  27.4 0.0 collective-permute-start.7
  27.4 0.0 copy-done.4
  27.4 0.4 collective-permute-start.11
  27.8 1.7 %collective-permute-start.10 = (bf16[32,4096]{1,0:T(8,128)(2,1)S(1)}, bf16[32,4096]{1,0:T(8,128)(2,1)S(1)}, u32[]{:S(2)}, u32[]{:S(2)}) collective-permute-start(bf16[32,4096]{1,0:T(8,128)(2,1)S(1)} %copy-done.4), channel_id=1, source_target_pairs={{0,4},{1,5},{2,6},{3,7},{4,0},{5,1},{6,2},{7,3},{8,12},{9,13},{10,... | collective-permute-start | bytes 786440 | tf_op jit(solution)/shard_map/ppermute | solution.py:517
  29.4 1.5 %collective-permute-start.9 = (bf16[32,4096]{1,0:T(8,128)(2,1)S(1)}, bf16[32,4096]{1,0:T(8,128)(2,1)S(1)}, u32[]{:S(2)}, u32[]{:S(2)}) collective-permute-start(bf16[32,4096]{1,0:T(8,128)(2,1)S(1)} %copy-done.4), channel_id=1, source_target_pairs={{0,2},{1,3},{2,0},{3,1},{4,6},{5,7},{6,4},{7,5},{8,10},{9,11},{10,... | collective-permute-start | bytes 786440 | tf_op jit(solution)/shard_map/ppermute | solution.py:517
  30.9 0.0 collective-permute-done.7.refs_8_.refs_19_
  30.9 0.0 collective-permute-start.8
  30.9 1.4 %collective-permute-done.8.refs_9_.refs_20_ = bf16[784,128]{1,0:T(8,128)(2,1)S(1)} collective-permute-done((bf16[784,128]{1,0:T(8,128)(2,1)S(1)}, bf16[784,128]{1,0:T(8,128)(2,1)S(1)}, u32[]{:S(2)}, u32[]{:S(2)}) %collective-permute-start.8) | collective-permute-done | bytes 200736 | tf_op jit(solution)/shard_map/ppermute | solution.py:517
  32.4 0.0 copy-start
  32.4 1.0 %copy-done = bf16[784,256]{1,0:T(8,128)(2,1)S(1)} copy-done((bf16[784,256]{1,0:T(8,128)(2,1)S(1)}, bf16[784,256]{1,0:T(8,128)(2,1)}, u32[]{:S(2)}) %copy-start) | copy-done | bytes 401432
  33.4 13.1 %gram_and_first_panels.1 = (f32[768,768]{1,0:T(8,128)S(1)}, f32[8,128]{1,0:T(8,128)S(1)}, f32[3,2,128,128]{3,2,1,0:T(8,128)S(1)}, f32[128,128]{1,0:T(8,128)S(1)}) custom-call(bf16[784,256]{1,0:T(8,128)(2,1)S(1)} %copy-done, bf16[784,256]{1,0:T(8,128)(2,1)S(1)} %collective-permute-done.2.refs_1_.refs_12_, ...), custom_call_target="tpu_custom_call" | custom-call | tf_op jit(solution)/shard_map/gram_and_first_panels/pallas_call | solution.py:324
  46.5 0.0 collective-permute-done.11
  46.5 0.0 collective-permute-done.10
  46.5 0.0 collective-permute-done.9
  46.5 0.0 collective-permute-done.12
  46.6 0.8 %fusion.1 = f32[128,256]{1,0:T(8,128)S(1)} fusion(bf16[128,4096]{1,0:T(8,128)(2,1)S(1)} %constant_dynamic-update-slice_fusion, bf16[256,4096]{1,0:T(8,128)(2,1)S(1)} %copy-done.3), kind=kOutput, calls=%fused_computation.6 | convolution fusion | flops 268435456 | bytes 3276800 | tf_op jit(solution)/shard_map/dot_general | solution.py:549
  47.5 1.0 %fusion.2 = f32[128,256]{1,0:T(8,128)S(1)} fusion(bf16[128,4096]{1,0:T(8,128)(2,1)S(1)} %constant_dynamic-update-slice_fusion, bf16[256,4096]{1,0:T(8,128)(2,1)S(1)} %collective-permute-done.12), kind=kOutput, calls=%fused_computation.7 | convolution fusion | flops 268435456 | bytes 3276800 | tf_op jit(solution)/shard_map/dot_general | solution.py:549
  48.5 0.0 copy-start.1
  48.5 0.0 copy-start.2
  48.6 0.4 collective-permute-start.15
  49.0 1.7 %collective-permute-start.14 = (f32[32,512]{1,0:T(8,128)S(1)}, f32[32,512]{1,0:T(8,128)S(1)}, u32[]{:S(2)}, u32[]{:S(2)}) collective-permute-start(f32[32,512]{1,0:T(8,128)S(1)} %get-tuple-element.56), channel_id=1, source_target_pairs={{0,4},{1,5},{2,6},{3,7},{4,0},{5,1},{6,2},{7,3},{8,12},{9,13},{10,... | collective-permute-start | bytes 196616 | tf_op jit(solution)/shard_map/ppermute | solution.py:517
  50.6 1.5 %collective-permute-start.13 = (f32[32,512]{1,0:T(8,128)S(1)}, f32[32,512]{1,0:T(8,128)S(1)}, u32[]{:S(2)}, u32[]{:S(2)}) collective-permute-start(f32[32,512]{1,0:T(8,128)S(1)} %get-tuple-element.57), channel_id=1, source_target_pairs={{0,2},{1,3},{2,0},{3,1},{4,6},{5,7},{6,4},{7,5},{8,10},{9,11},{10,... | collective-permute-start | bytes 196616 | tf_op jit(solution)/shard_map/ppermute | solution.py:517
  52.1 3.9 %middle_panels.1 = (f32[512,512]{1,0:T(8,128)S(1)}, f32[1,2,128,128]{3,2,1,0:T(8,128)S(1)}, f32[128,128]{1,0:T(8,128)S(1)}) custom-call(f32[768,768]{1,0:T(8,128)S(1)} %get-tuple-element.49.start_ref.refs_6_, f32[3,2,128,128]{3,2,1,0:T(8,128)S(1)} %get-tuple-element.50.early_ref.refs_7_, f32[128,128]{1,0:T(8,128)S(1)} %get-tuple-element.51.start_next_ref), custom_call_target="tpu_custom_call" | custom-call | tf_op jit(solution)/shard_map/middle_panels/pallas_call | solution.py:370
  56.0 0.0 collective-permute-done.15.refs_4_
  56.0 0.0 collective-permute-done.14.refs_3_
  56.1 0.0 collective-permute-done.13.refs_2_
  56.1 0.0 copy-done.1
  56.1 0.0 copy-done.2
  56.1 10.1 %last_panels_and_solution.1 = bf16[32,4096]{1,0:T(8,128)(2,1)} custom-call(s32[64]{0:T(128)S(1)} %copy-done.2, f32[32,512]{1,0:T(8,128)S(1)} %get-tuple-element.58.refs_1_, f32[32,512]{1,0:T(8,128)S(1)} %collective-permute-done.13.refs_2_, f32[32,512]{1,0:T(8,128)S(1)} %collective-permute-done.14.refs_3_, f32[32,512]{1,0:T(8,128)S(1)} %collective-permute-done.15.refs_4_, ...), custom_call_target="tpu_custom_call" | custom-call | tf_op jit(solution)/shard_map/last_panels_and_solution/pallas_call | solution.py:492
  (8 shorter events, 0.1 us)
Async XLA Ops:
  0.0 3.9 %copy-start.3 = (bf16[256,4096]{1,0:T(8,128)(2,1)S(1)}, bf16[256,4096]{1,0:T(8,128)(2,1)}, u32[]{:S(2)}) copy-start(bf16[256,4096]{1,0:T(8,128)(2,1)} %tokens_ref.1) | copy-start | bytes 6291460
  0.0 27.4 %copy-start.4 = (bf16[32,4096]{1,0:T(8,128)(2,1)S(1)}, bf16[32,4096]{1,0:T(8,128)(2,1)}, u32[]{:S(2)}) copy-start(bf16[32,4096]{1,0:T(8,128)(2,1)} %param.4) | copy-start | bytes 786436
  3.9 42.7 %collective-permute-start.12 = (bf16[256,4096]{1,0:T(8,128)(2,1)S(1)}, bf16[256,4096]{1,0:T(8,128)(2,1)S(1)}, u32[]{:S(2)}, u32[]{:S(2)}) collective-permute-start(bf16[256,4096]{1,0:T(8,128)(2,1)S(1)} %copy-done.3), channel_id=1, source_target_pairs={{0,1},{1,0},{2,3},{3,2},{4,5},{5,4},{6,7},{7,6},{8,9},{9,8},{10,11... | collective-permute-start | bytes 6291464 | tf_op jit(solution)/shard_map/ppermute | solution.py:517
  4.4 4.5 %collective-permute-start.2 = (bf16[784,256]{1,0:T(8,128)(2,1)}, bf16[784,256]{1,0:T(8,128)(2,1)S(1)}, u32[]{:S(2)}, u32[]{:S(2)}) collective-permute-start(bf16[784,256]{1,0:T(8,128)(2,1)} %select_kept.1.refs_0_.refs_11_), channel_id=1, source_target_pairs={{0,1},{1,0},{2,3},{3,2},{4,5},{5,4},{6,7},{7,6},{8,9},{9,8},{10,11... | collective-permute-start | bytes 1204232 | tf_op jit(solution)/shard_map/ppermute | solution.py:517
  4.5 12.7 %collective-permute-start.1 = (bf16[784,256]{1,0:T(8,128)(2,1)}, bf16[784,256]{1,0:T(8,128)(2,1)S(1)}, u32[]{:S(2)}, u32[]{:S(2)}) collective-permute-start(bf16[784,256]{1,0:T(8,128)(2,1)} %select_kept.1.refs_0_.refs_11_), channel_id=1, source_target_pairs={{0,4},{1,5},{2,6},{3,7},{4,0},{5,1},{6,2},{7,3},{8,12},{9,13},{10,... | collective-permute-start | bytes 1204232 | tf_op jit(solution)/shard_map/ppermute | solution.py:517
  7.4 11.2 %collective-permute-start = (bf16[784,256]{1,0:T(8,128)(2,1)}, bf16[784,256]{1,0:T(8,128)(2,1)S(1)}, u32[]{:S(2)}, u32[]{:S(2)}) collective-permute-start(bf16[784,256]{1,0:T(8,128)(2,1)} %select_kept.1.refs_0_.refs_11_), channel_id=1, source_target_pairs={{0,2},{1,3},{2,0},{3,1},{4,6},{5,7},{6,4},{7,5},{8,10},{9,11},{10,... | collective-permute-start | bytes 1204232 | tf_op jit(solution)/shard_map/ppermute | solution.py:517
  18.6 8.7 %collective-permute-start.5 = (bf16[784,256]{1,0:T(8,128)(2,1)S(1)}, bf16[784,256]{1,0:T(8,128)(2,1)S(1)}, u32[]{:S(2)}, u32[]{:S(2)}) collective-permute-start(bf16[784,256]{1,0:T(8,128)(2,1)S(1)} %collective-permute-done.refs_2_.refs_13_), channel_id=1, source_target_pairs={{0,1},{1,0},{2,3},{3,2},{4,5},{5,4},{6,7},{7,6},{8,9},{9,8},{10,11... | collective-permute-start | bytes 1204232 | tf_op jit(solution)/shard_map/ppermute | solution.py:517
  18.6 8.7 %collective-permute-start.6 = (bf16[784,256]{1,0:T(8,128)(2,1)S(1)}, bf16[784,256]{1,0:T(8,128)(2,1)S(1)}, u32[]{:S(2)}, u32[]{:S(2)}) collective-permute-start(bf16[784,256]{1,0:T(8,128)(2,1)S(1)} %collective-permute-done.1.refs_4_.refs_15_), channel_id=1, source_target_pairs={{0,1},{1,0},{2,3},{3,2},{4,5},{5,4},{6,7},{7,6},{8,9},{9,8},{10,11... | collective-permute-start | bytes 1204232 | tf_op jit(solution)/shard_map/ppermute | solution.py:517
  19.2 7.0 %collective-permute-start.4 = (bf16[784,128]{1,0:T(8,128)(2,1)S(1)}, bf16[784,128]{1,0:T(8,128)(2,1)S(1)}, u32[]{:S(2)}, u32[]{:S(2)}) collective-permute-start(bf16[784,128]{1,0:T(8,128)(2,1)S(1)} %slice.19), channel_id=1, source_target_pairs={{0,2},{1,3},{2,0},{3,1},{4,6},{5,7},{6,4},{7,5},{8,10},{9,11},{10,... | collective-permute-start | bytes 602120 | tf_op jit(solution)/shard_map/ppermute | solution.py:517
  20.7 6.6 %collective-permute-start.3 = (bf16[784,128]{1,0:T(8,128)(2,1)S(1)}, bf16[784,128]{1,0:T(8,128)(2,1)S(1)}, u32[]{:S(2)}, u32[]{:S(2)}) collective-permute-start(bf16[784,128]{1,0:T(8,128)(2,1)S(1)} %slice.18), channel_id=1, source_target_pairs={{0,4},{1,5},{2,6},{3,7},{4,0},{5,1},{6,2},{7,3},{8,12},{9,13},{10,... | collective-permute-start | bytes 602120 | tf_op jit(solution)/shard_map/ppermute | solution.py:517
  27.4 3.6 %collective-permute-start.7 = (bf16[784,128]{1,0:T(8,128)(2,1)S(1)}, bf16[784,128]{1,0:T(8,128)(2,1)S(1)}, u32[]{:S(2)}, u32[]{:S(2)}) collective-permute-start(bf16[784,128]{1,0:T(8,128)(2,1)S(1)} %collective-permute-done.3.refs_6_.refs_17_), channel_id=1, source_target_pairs={{0,1},{1,0},{2,3},{3,2},{4,5},{5,4},{6,7},{7,6},{8,9},{9,8},{10,11... | collective-permute-start | bytes 602120 | tf_op jit(solution)/shard_map/ppermute | solution.py:517
  27.4 19.1 %collective-permute-start.11 = (bf16[32,4096]{1,0:T(8,128)(2,1)S(1)}, bf16[32,4096]{1,0:T(8,128)(2,1)S(1)}, u32[]{:S(2)}, u32[]{:S(2)}) collective-permute-start(bf16[32,4096]{1,0:T(8,128)(2,1)S(1)} %copy-done.4), channel_id=1, source_target_pairs={{0,6},{1,7},{2,4},{3,5},{4,2},{5,3},{6,0},{7,1},{8,14},{9,15},{10,... | collective-permute-start | bytes 786440 | tf_op jit(solution)/shard_map/ppermute | solution.py:517
  27.8 18.7 %collective-permute-start.10 = (bf16[32,4096]{1,0:T(8,128)(2,1)S(1)}, bf16[32,4096]{1,0:T(8,128)(2,1)S(1)}, u32[]{:S(2)}, u32[]{:S(2)}) collective-permute-start(bf16[32,4096]{1,0:T(8,128)(2,1)S(1)} %copy-done.4), channel_id=1, source_target_pairs={{0,4},{1,5},{2,6},{3,7},{4,0},{5,1},{6,2},{7,3},{8,12},{9,13},{10,... | collective-permute-start | bytes 786440 | tf_op jit(solution)/shard_map/ppermute | solution.py:517
  29.4 17.1 %collective-permute-start.9 = (bf16[32,4096]{1,0:T(8,128)(2,1)S(1)}, bf16[32,4096]{1,0:T(8,128)(2,1)S(1)}, u32[]{:S(2)}, u32[]{:S(2)}) collective-permute-start(bf16[32,4096]{1,0:T(8,128)(2,1)S(1)} %copy-done.4), channel_id=1, source_target_pairs={{0,2},{1,3},{2,0},{3,1},{4,6},{5,7},{6,4},{7,5},{8,10},{9,11},{10,... | collective-permute-start | bytes 786440 | tf_op jit(solution)/shard_map/ppermute | solution.py:517
  30.9 1.4 %collective-permute-start.8 = (bf16[784,128]{1,0:T(8,128)(2,1)S(1)}, bf16[784,128]{1,0:T(8,128)(2,1)S(1)}, u32[]{:S(2)}, u32[]{:S(2)}) collective-permute-start(bf16[784,128]{1,0:T(8,128)(2,1)S(1)} %collective-permute-done.4.refs_7_.refs_18_), channel_id=1, source_target_pairs={{0,1},{1,0},{2,3},{3,2},{4,5},{5,4},{6,7},{7,6},{8,9},{9,8},{10,11... | collective-permute-start | bytes 602120 | tf_op jit(solution)/shard_map/ppermute | solution.py:517
  32.4 1.0 %copy-start = (bf16[784,256]{1,0:T(8,128)(2,1)S(1)}, bf16[784,256]{1,0:T(8,128)(2,1)}, u32[]{:S(2)}) copy-start(bf16[784,256]{1,0:T(8,128)(2,1)} %select_kept.1.refs_0_.refs_11_) | copy-start | bytes 1204228
  48.5 7.6 %copy-start.1 = (bf16[784,256]{1,0:T(8,128)(2,1)S(1)}, bf16[784,256]{1,0:T(8,128)(2,1)}, u32[]{:S(2)}) copy-start(bf16[784,256]{1,0:T(8,128)(2,1)} %select_kept.1.refs_0_.refs_11_) | copy-start | bytes 1204228
  48.5 7.6 %copy-start.2 = (s32[64]{0:T(128)S(1)}, s32[64]{0:T(128)}, u32[]{:S(2)}) copy-start(s32[64]{0:T(128)} %refs_0_.1) | copy-start | bytes 772
  48.6 7.5 %collective-permute-start.15 = (f32[32,512]{1,0:T(8,128)S(1)}, f32[32,512]{1,0:T(8,128)S(1)}, u32[]{:S(2)}, u32[]{:S(2)}) collective-permute-start(f32[32,512]{1,0:T(8,128)S(1)} %get-tuple-element.55), channel_id=1, source_target_pairs={{0,6},{1,7},{2,4},{3,5},{4,2},{5,3},{6,0},{7,1},{8,14},{9,15},{10,... | collective-permute-start | bytes 196616 | tf_op jit(solution)/shard_map/ppermute | solution.py:517
  49.0 7.1 %collective-permute-start.14 = (f32[32,512]{1,0:T(8,128)S(1)}, f32[32,512]{1,0:T(8,128)S(1)}, u32[]{:S(2)}, u32[]{:S(2)}) collective-permute-start(f32[32,512]{1,0:T(8,128)S(1)} %get-tuple-element.56), channel_id=1, source_target_pairs={{0,4},{1,5},{2,6},{3,7},{4,0},{5,1},{6,2},{7,3},{8,12},{9,13},{10,... | collective-permute-start | bytes 196616 | tf_op jit(solution)/shard_map/ppermute | solution.py:517
  50.6 5.4 %collective-permute-start.13 = (f32[32,512]{1,0:T(8,128)S(1)}, f32[32,512]{1,0:T(8,128)S(1)}, u32[]{:S(2)}, u32[]{:S(2)}) collective-permute-start(f32[32,512]{1,0:T(8,128)S(1)} %get-tuple-element.57), channel_id=1, source_target_pairs={{0,2},{1,3},{2,0},{3,1},{4,6},{5,7},{6,4},{7,5},{8,10},{9,11},{10,... | collective-permute-start | bytes 196616 | tf_op jit(solution)/shard_map/ppermute | solution.py:517
